TPU v7x, 32 devices: a whole 2x2x4 slice. The times are simulated.
32 devices in a mesh: fsdp: 2 (over x), dp: 4 (over z), owner: 4 (over y, core).
Axes of the slice: x: 2, y: 2, z: 4, core: 2. Of those that a mesh axis runs over, the one named last changes fastest.
Arguments:
- hidden: bfloat16 [32, 256, 4096], P(('fsdp', 'dp', 'owner')), may hold values from -6 to 6
- norm_gain: float32 [4096], replicated, may hold values from 0.1 to 1.9
- query_weight: bfloat16 [4096, 2048], P(('fsdp', 'dp')), may hold values from -0.09375 to 0.09375
- key_value_weight: bfloat16 [4096, 1024], P(('fsdp', 'dp')), may hold values from -0.09375 to 0.09375
- lengths: int32 [32], P(('fsdp', 'dp', 'owner')), may hold values from 128 to 256, as said below
- cotangent: bfloat16 [32, 256, 2048], P(('fsdp', 'dp', 'owner')), may hold values from -6 to 6
- cartridge: float32 [512, 1024], P('owner'), may hold values from -48 to 48
- adam_first_moment: float32 [512, 1024], P('owner'), may hold values from -6 to 6
- adam_second_moment: float32 [512, 1024], P('owner'), may hold values from 0.01 to 1
Outputs:
- attention_out: bfloat16 [32, 256, 2048], P(('fsdp', 'dp', 'owner'))
- new_cartridge: float32 [512, 1024], P('owner')
- new_first: float32 [512, 1024], P('owner')
- new_second: float32 [512, 1024], P('owner')
Inputs may be any that keep to these rules, and one draw needn't show every extreme that they name: `lengths`: each conversation's live tokens are its first rows; the rows after them are padding; some conversation is full.
All inputs are finite; a program needn't handle non-finite values.
Results may differ from a plain program's by a relative error of at most 0.008.
The roundings to bfloat16 on the way count: a program that leaves them out, or rounds other values in their place, can miss the bound.
Values may be sent and summed in bfloat16 or wider, within the bound.
A program may use at most 128 MiB of HBM per device.

v0:
```python
import jax
import jax.numpy as jnp
from jax import lax
from jax.sharding import PartitionSpec as P

HEAD_SIZE = 128
QUERY_HEADS = 16
KEY_VALUE_HEADS = 4
STEP = 50


def rotary_heads(values, offset):
    sequence_rows = values.shape[0]
    half_size = values.shape[2] // 2
    exponent = jnp.arange(half_size, dtype=jnp.float32) * (2.0 / values.shape[2])
    inverse = jnp.power(jnp.float32(500000.0), -exponent)
    position = (offset + jnp.arange(sequence_rows)).astype(jnp.float32)
    angles = position[:, None] * inverse[None, :]
    cosine = jnp.cos(angles)[:, None, :]
    sine = jnp.sin(angles)[:, None, :]
    first_half = values[..., :half_size]
    second_half = values[..., half_size:]
    return jnp.concatenate(
        [first_half * cosine - second_half * sine, second_half * cosine + first_half * sine],
        axis=-1,
    )


def adam_update(current, moment_one, moment_two, prefix_gradient):
    one_new = 0.9 * moment_one + 0.1 * prefix_gradient
    two_new = 0.999 * moment_two + 0.001 * prefix_gradient * prefix_gradient
    one_fix = 1.0 - 0.9**STEP
    two_fix = 1.0 - 0.999**STEP
    updated = current - 0.02 * (one_new / one_fix) / (jnp.sqrt(two_new / two_fix) + 1e-08)
    return (updated, one_new, two_new)


def add_rows(pieces, features):
    return (
        jnp.dot(features, pieces[0], preferred_element_type=jnp.float32),
        jnp.dot(features, pieces[1], preferred_element_type=jnp.float32),
    )


def on_device(
    hidden,
    norm_gain,
    query_weight,
    key_value_weight,
    lengths,
    cotangent,
    cartridge,
    adam_first_moment,
    adam_second_moment,
):
    sequence_rows = hidden.shape[1]
    query_group_size = QUERY_HEADS // KEY_VALUE_HEADS
    score_scale = HEAD_SIZE ** (-0.5)
    states = hidden[0].astype(jnp.float32)
    normed = (
        states * lax.rsqrt(jnp.mean(states * states, axis=1, keepdims=True) + 1e-05) * norm_gain
    ).astype(jnp.bfloat16)
    exchanged = lax.all_to_all(normed[None], "fsdp", split_axis=2, concat_axis=0, tiled=True)
    pair_rows = exchanged.reshape(-1, exchanged.shape[2])
    part_query, part_keyval = add_rows(
        (
            lax.all_gather(query_weight, "dp", axis=0, tiled=True),
            lax.all_gather(key_value_weight, "dp", axis=0, tiled=True),
        ),
        pair_rows,
    )
    proj_query, project_key_value = (
        lax.psum_scatter(part_query, "fsdp", scatter_dimension=0, tiled=True),
        lax.psum_scatter(part_keyval, "fsdp", scatter_dimension=0, tiled=True),
    )
    shard_rows = cartridge.shape[0]
    prefix_length = shard_rows * lax.axis_size("owner")
    query_rows = rotary_heads(
        proj_query.reshape(sequence_rows, QUERY_HEADS, HEAD_SIZE), prefix_length
    ).astype(jnp.bfloat16)
    sequence_keys = rotary_heads(
        project_key_value[:, : KEY_VALUE_HEADS * HEAD_SIZE].reshape(
            sequence_rows, KEY_VALUE_HEADS, HEAD_SIZE
        ),
        prefix_length,
    ).astype(jnp.bfloat16)
    sequence_values = (
        project_key_value[:, KEY_VALUE_HEADS * HEAD_SIZE :]
        .reshape(sequence_rows, KEY_VALUE_HEADS, HEAD_SIZE)
        .astype(jnp.bfloat16)
    )
    gathered_rows = lax.all_gather(cartridge.astype(jnp.bfloat16), "owner", axis=0, tiled=True)
    cartridge_keys = gathered_rows[:, : KEY_VALUE_HEADS * HEAD_SIZE].reshape(
        prefix_length, KEY_VALUE_HEADS, HEAD_SIZE
    )
    cartridge_values = gathered_rows[:, KEY_VALUE_HEADS * HEAD_SIZE :].reshape(
        prefix_length, KEY_VALUE_HEADS, HEAD_SIZE
    )
    grouped_heads = query_rows.reshape(sequence_rows, KEY_VALUE_HEADS, query_group_size, HEAD_SIZE)
    pre_scores = (
        jnp.einsum(
            "shgd,phd->hgsp", grouped_heads, cartridge_keys, preferred_element_type=jnp.float32
        )
        * score_scale
    )
    own_scores = (
        jnp.einsum(
            "shgd,thd->hgst", grouped_heads, sequence_keys, preferred_element_type=jnp.float32
        )
        * score_scale
    )
    causal = jnp.arange(sequence_rows)[:, None] >= jnp.arange(sequence_rows)[None, :]
    own_scores = jnp.where(causal, own_scores, -jnp.inf)
    highest = jnp.maximum(
        jnp.max(pre_scores, axis=-1, keepdims=True), jnp.max(own_scores, axis=-1, keepdims=True)
    )
    pre_exp = jnp.exp(pre_scores - highest)
    own_exp = jnp.exp(own_scores - highest)
    denominator = jnp.sum(pre_exp, axis=-1, keepdims=True) + jnp.sum(
        own_exp, axis=-1, keepdims=True
    )
    pre_probs = pre_exp / denominator
    pre_low = pre_probs.astype(jnp.bfloat16)
    own_low = (own_exp / denominator).astype(jnp.bfloat16)
    attended = jnp.einsum(
        "hgsp,phd->shgd", pre_low, cartridge_values, preferred_element_type=jnp.float32
    )
    attended = attended + jnp.einsum(
        "hgst,thd->shgd", own_low, sequence_values, preferred_element_type=jnp.float32
    )
    active_rows = (jnp.arange(sequence_rows) < lengths[0])[:, None, None, None]
    attention_out = jnp.where(active_rows, attended, 0.0).astype(jnp.bfloat16)
    upstream_gradient = jnp.where(
        active_rows,
        cotangent[0].reshape(sequence_rows, KEY_VALUE_HEADS, query_group_size, HEAD_SIZE),
        0.0,
    )
    delta = jnp.einsum(
        "shgd,shgd->hgs", upstream_gradient, attention_out, preferred_element_type=jnp.float32
    )
    dprob = jnp.einsum(
        "shgd,phd->hgsp", upstream_gradient, cartridge_values, preferred_element_type=jnp.float32
    )
    dscore = (pre_probs * (dprob - delta[..., None])).astype(jnp.bfloat16)
    gradient_keys = (
        jnp.einsum("hgsp,shgd->phd", dscore, grouped_heads, preferred_element_type=jnp.float32)
        * score_scale
    )
    gradient_values = jnp.einsum(
        "hgsp,shgd->phd", pre_low, upstream_gradient, preferred_element_type=jnp.float32
    )
    prefix_gradient = jnp.concatenate(
        [
            gradient_keys.reshape(prefix_length, KEY_VALUE_HEADS * HEAD_SIZE),
            gradient_values.reshape(prefix_length, KEY_VALUE_HEADS * HEAD_SIZE),
        ],
        axis=1,
    )
    summed = lax.psum(prefix_gradient, ("fsdp", "dp", "owner"))
    owned_sum = lax.dynamic_slice_in_dim(
        summed, lax.axis_index("owner") * shard_rows, shard_rows, 0
    )
    new_cartridge, new_first, new_second = adam_update(
        cartridge, adam_first_moment, adam_second_moment, owned_sum
    )
    return (
        attention_out.reshape(1, sequence_rows, QUERY_HEADS * HEAD_SIZE),
        new_cartridge,
        new_first,
        new_second,
    )


def solution(mesh):
    placed = (
        P(("fsdp", "dp", "owner"), None, None),
        P(),
        P(("fsdp", "dp"), None),
        P(("fsdp", "dp"), None),
        P(("fsdp", "dp", "owner")),
        P(("fsdp", "dp", "owner"), None, None),
        P("owner", None),
        P("owner", None),
        P("owner", None),
    )
    return jax.shard_map(
        on_device,
        mesh=mesh,
        in_specs=placed,
        out_specs=(
            P(("fsdp", "dp", "owner"), None, None),
            P("owner", None),
            P("owner", None),
            P("owner", None),
        ),
        check_vma=False,
    )
```

profile of v0, /device:TPU:0, one launch (start us, length us, event | category | flops | bytes accessed | tf_op | source)
XLA Modules:
  0.0 526.0 jit_solution(3117788285064798440)
XLA Ops:
  9.3 2.2 fusion.7
  11.5 7.4 %copy.72 = bf16[1,256,4096]{1,0,2:T(2,128)(2,1)} copy(bf16[1,256,4096]{2,1,0:T(8,128)(2,1)S(1)} %fusion.7) | data formatting | bytes 4194304 | tf_op jit(solution)/shard_map/convert_element_type | solution.py:62
  19.4 21.6 %reduce.3 = bf16[4096,256]{1,0:T(8,128)(2,1)S(1)} reduce(bf16[4096,1,256]{2,1,0:T(2,128)(2,1)} %bitcast.114, bf16[]{:T(256)} %broadcast.90), dimensions={1}, to_apply=%bitcast.98.reduce_sub_computation | reduce | bytes 4194306
  41.0 1.6 reshape.157
  42.6 4.2 all-to-all-start
  47.8 24.9 %all-to-all-done = bf16[2,2,262144]{2,1,0:T(2,128)(2,1)S(1)} async-done(((bf16[2,2,262144]{2,1,0:T(2,128)(2,1)}), bf16[2,2,262144]{2,1,0:T(2,128)(2,1)S(1)}, u32[]{:S(2)}, u32[]{:S(2)}) %all-to-all-start) | async-done | bytes 2097184 | tf_op jit(solution)/shard_map/all_to_all | solution.py:63
  72.7 3.1 reshape.158
  75.8 2.5 copy.111
  78.3 2.5 copy.73
  80.8 12.3 %all-gather.8.cloned.1.call-done = bf16[2048,1024]{1,0:T(8,128)(2,1)} async-done(((bf16[512,1024]{1,0:T(8,128)(2,1)}), bf16[2048,1024]{1,0:T(8,128)(2,1)}) %all-gather.8.cloned.1.call-update) | async-done | bytes 4194320 | tf_op jit(solution)/shard_map/all_gather | solution.py:68
  93.1 6.6 %fusion.52 = f32[512,1024]{1,0:T(8,128)} fusion(bf16[512,2048]{1,0:T(8,128)(2,1)} %bitcast.125, bf16[2048,1024]{1,0:T(8,128)(2,1)} %all-gather.8.cloned.1.call-done), kind=kOutput, calls=%fused_computation.67 | convolution fusion | flops 2147483648 | bytes 8388608 | tf_op jit(solution)/shard_map/dot_general | solution.py:41
  99.8 143.1 %all-gather.4.cloned.1.call-done = bf16[2048,2048]{1,0:T(8,128)(2,1)} async-done(((bf16[512,2048]{1,0:T(8,128)(2,1)}), bf16[2048,2048]{1,0:T(8,128)(2,1)}) %all-gather.4.cloned.1.call-update) | async-done | bytes 8388624 | tf_op jit(solution)/shard_map/all_gather | solution.py:67
  242.9 9.4 %fusion.51 = f32[512,2048]{1,0:T(8,128)} fusion(bf16[512,2048]{1,0:T(8,128)(2,1)S(1)} %bitcast.126, bf16[2048,2048]{1,0:T(8,128)(2,1)} %all-gather.4.cloned.1.call-done), kind=kOutput, calls=%fused_computation.66 | convolution fusion | flops 4294967296 | bytes 14680064 | tf_op jit(solution)/shard_map/dot_general | solution.py:40
  253.5 1.3 copy.82
  256.0 4.1 all-gather.6.cloned.1.call-done
  260.1 2.1 fusion.49
  262.2 31.9 %reduce-scatter.5.cloned.1.call-done = f32[256,1024]{1,0:T(8,128)} async-done(((f32[512,1024]{1,0:T(8,128)}), f32[256,1024]{1,0:T(8,128)}) %reduce-scatter.5.cloned.1.call-update) | async-done | bytes 1048592 | tf_op jit(solution)/shard_map/reduce_scatter | solution.py:74
  298.4 52.2 %reduce-scatter.3.cloned.1.call-done = f32[256,2048]{1,0:T(8,128)} async-done(((f32[512,2048]{1,0:T(8,128)}), f32[256,2048]{1,0:T(8,128)}) %reduce-scatter.3.cloned.1.call-update) | async-done | bytes 2097168 | tf_op jit(solution)/shard_map/reduce_scatter | solution.py:73
  350.6 2.0 copy.114
  354.0 1.5 bitcast_reduce_fusion
  355.5 1.4 fusion.14
  357.9 2.2 fusion.4
  360.1 1.4 fusion.22
  361.6 3.5 fusion.18
  365.0 4.0 fusion.15
  369.0 9.1 %fusion.28 = f32[4,128,512]{2,1,0:T(8,128)} fusion(f32[4,4,256]{2,1,0:T(4,128)S(1)} %get-tuple-element.41, bf16[512,4,128,1]{0,2,3,1:T(8,128)(2,1)S(1)} %bitcast.134, bf16[256,4,4,128]{0,3,2,1:T(8,128)(2,1)} %bitcast.127, pred[256]{0:T(512)(128)(4,1)S(1)} %iota_compare_fusion.1, bf16[256,4,4,64]{3,0,2,1:T(8,128)(2,1)S(1)} %bitcast.121, ...), kind=kOutput, calls=%fused_computation.35 | convolution fusion | flops 1089208320 | bytes 12108032 | tf_op jit(solution)/shard_map/hgsp,shgd->phd/dot_general | solution.py:146
  378.1 1.6 copy.86
  379.7 1.6 copy.87
  381.3 1.5 pad_maximum_fusion
  382.8 2.3 copy.88
  385.1 131.6 %all-reduce.2.cloned.1.call-done = f32[512,1024]{1,0:T(8,128)} async-done(((f32[512,1024]{1,0:T(8,128)}), f32[512,1024]{1,0:T(8,128)}) %all-reduce.2.cloned.1.call-update) | async-done | bytes 2097168 | tf_op jit(solution)/shard_map/psum | solution.py:159
  516.7 2.4 divide_subtract_fusion
  (57 shorter events, 12.0 us)
Async XLA Ops:
  7.2 1.6 copy-start.1
  7.2 2.1 copy-start.11
  7.2 85.9 %all-gather.8.cloned.1.call-start = ((), (), s32[]{:S(2)}) async-start(), calls=%async_computation.6 | async-start | bytes 5242880 | tf_op jit(solution)/shard_map/all_gather | solution.py:68
  7.9 234.9 %all-gather.4.cloned.1.call-start = ((), (), s32[]{:S(2)}) async-start(), calls=%async_computation.3 | async-start | bytes 10485760 | tf_op jit(solution)/shard_map/all_gather | solution.py:67
  41.0 5.9 %copy-start.3 = (f32[128,1024]{1,0:T(8,128)S(1)}, f32[128,1024]{1,0:T(8,128)}, u32[]{:S(2)}) copy-start(f32[128,1024]{1,0:T(8,128)} %param.15) | copy-start | bytes 1572868
  42.6 30.1 %all-to-all-start = ((bf16[2,2,262144]{2,1,0:T(2,128)(2,1)}), bf16[2,2,262144]{2,1,0:T(2,128)(2,1)S(1)}, u32[]{:S(2)}, u32[]{:S(2)}) async-start(bf16[2,2,262144]{2,1,0:T(2,128)(2,1)} %reshape.157), calls=%async_computation | async-start | bytes 4194304 | tf_op jit(solution)/shard_map/all_to_all | solution.py:63
  46.8 213.2 %all-gather.6.cloned.1.call-start = ((), (), s32[]{:S(2)}) async-start(), calls=%async_computation.5 | async-start | bytes 1310720 | tf_op jit(solution)/shard_map/all_gather | solution.py:92
  47.7 246.3 %reduce-scatter.5.cloned.1.call-start = ((), (), s32[]{:S(2)}) async-start(), calls=%async_computation.7 | async-start | bytes 3145728 | tf_op jit(solution)/shard_map/reduce_scatter | solution.py:74
  93.1 149.8 %copy-start.2 = (bf16[2,1,256,2048]{3,2,0,1:T(8,128)(2,1)S(1)}, bf16[2,1,256,2048]{3,2,0,1:T(8,128)(2,1)}, u32[]{:S(2)}) copy-start(bf16[2,1,256,2048]{3,2,0,1:T(8,128)(2,1)} %copy.73) | copy-start | bytes 6291460
  99.7 250.9 %reduce-scatter.3.cloned.1.call-start = ((), (), s32[]{:S(2)}) async-start(), calls=%async_computation.4 | async-start | bytes 6291456 | tf_op jit(solution)/shard_map/reduce_scatter | solution.py:73
  252.2 1.2 copy-start.4
  252.3 264.5 %all-reduce.2.cloned.1.call-start = ((), (), s32[]{:S(2)}) async-start(), calls=%async_computation.8 | async-start | bytes 4194304 | tf_op jit(solution)/shard_map/psum | solution.py:159
  353.9 1.6 copy-start.6
  355.5 9.5 %copy-start = (f32[4,256,4,512]{3,1,2,0:T(8,128)}, f32[4,256,4,512]{3,1,2,0:T(8,128)S(1)}, u32[]{:S(2)}) copy-start(f32[4,256,4,512]{3,1,2,0:T(8,128)S(1)} %get-tuple-element.38) | copy-start | bytes 25165828
  357.9 2.2 copy-start.10
  360.1 1.5 copy-start.5
  361.6 3.5 copy-start.9
  381.3 135.5 %copy-start.7 = (f32[128,1024]{1,0:T(8,128)S(1)}, f32[128,1024]{1,0:T(8,128)}, u32[]{:S(2)}) copy-start(f32[128,1024]{1,0:T(8,128)} %param.16) | copy-start | bytes 1572868
  382.8 134.0 %copy-start.8 = (f32[128,1024]{1,0:T(8,128)S(1)}, f32[128,1024]{1,0:T(8,128)}, u32[]{:S(2)}) copy-start(f32[128,1024]{1,0:T(8,128)} %param.17) | copy-start | bytes 1572868
Sparse Core Ops, SparseCore 0:
  9.6 83.4 all-gather.7
  94.7 148.1 all-gather.3
  245.0 15.0 all-gather.5
  262.2 31.8 reduce-scatter.4
  296.3 54.3 reduce-scatter.2
  382.9 133.7 all-reduce.1
where the time goes:
time: 527 us; the launch traced here: 526 us
  waiting for transfers between devices  402 us (76%)
  matrix products  37 us (7%)
  local copies, waits for them, and re-layouts  34.3 us (7%)
  other arithmetic  33.5 us (6%)
  between operations  15 us (3%)
    all_gather x1, waiting for transfers between devices, on_device(): lax.all_gather(query_weight, 'dp', axis=0, tiled=True)  143 us
    psum x1, waiting for transfers between devices, on_device(): summed = lax.psum(prefix_gradient, ('fsdp', 'dp', 'owner'))  132 us
    reduce_scatter x1, waiting for transfers between devices, on_device(): lax.psum_scatter(part_query, 'fsdp', scatter_dimension=0, tiled=True)  52.2 us
    reduce_scatter x1, waiting for transfers between devices, on_device(): lax.psum_scatter(part_keyval, 'fsdp', scatter_dimension=0, tiled=True)  31.9 us
    all_to_all x1, waiting for transfers between devices, on_device(): lax.all_to_all(normed[None], 'fsdp', split_axis=2, concat_axis=0, tiled=T...  24.9 us
    unnamed x1, other arithmetic  21.6 us
    unnamed x32, local copies, waits for them, and re-layouts  15.3 us
    all_gather x1, waiting for transfers between devices, on_device(): lax.all_gather(key_value_weight, 'dp', axis=0, tiled=True)  12.3 us
  transfers between devices with their start and end apart: 7, of which 7 were waited for; matrix products, arithmetic and copies ran while one was open for 13% of the time, Pallas kernels for 0%

commit v1 on v0

v1 whole, which is shorter than its diff:
```python
import functools

import jax
import jax.numpy as jnp
from jax import lax
from jax.experimental import pallas as pl
from jax.experimental.pallas import tpu as pltpu
from jax.sharding import PartitionSpec as P

HEAD_SIZE = 128
QUERY_HEADS = 16
KEY_VALUE_HEADS = 4
GROUP = QUERY_HEADS // KEY_VALUE_HEADS
STEP = 50
LOG2E = 1.4426950408889634


def angle_tables(sequence_rows, offset):
    half_size = HEAD_SIZE // 2
    exponent = jnp.arange(half_size, dtype=jnp.float32) * (2.0 / HEAD_SIZE)
    inverse = jnp.power(jnp.float32(500000.0), -exponent)
    position = (offset + jnp.arange(sequence_rows)).astype(jnp.float32)
    angles = position[:, None] * inverse[None, :]
    cosine, sine = jnp.cos(angles), jnp.sin(angles)
    return (
        jnp.concatenate([cosine, cosine], axis=1),
        jnp.concatenate([-sine, sine], axis=1),
    )


def adam_update(current, moment_one, moment_two, prefix_gradient):
    one_new = 0.9 * moment_one + 0.1 * prefix_gradient
    two_new = 0.999 * moment_two + 0.001 * prefix_gradient * prefix_gradient
    one_fix = 1.0 - 0.9**STEP
    two_fix = 1.0 - 0.999**STEP
    updated = current - 0.02 * (one_new / one_fix) / (jnp.sqrt(two_new / two_fix) + 1e-08)
    return (updated, one_new, two_new)


def dot_f32(left, right, left_dim, right_dim):
    return lax.dot_general(
        left, right, (((left_dim,), (right_dim,)), ((), ())), preferred_element_type=jnp.float32
    )


def attention_kernel(
    length_ref, cos_ref, sin_ref, pq_ref, pk_ref, pv_ref, keys_ref, values_ref, cot_ref,
    out_ref, gk_ref, gv_ref,
):
    rows = pq_ref.shape[0]
    prefix_length = keys_ref.shape[0]
    scale = HEAD_SIZE ** (-0.5)
    cos, sin = cos_ref[...], sin_ref[...]

    def rope(v):
        return (v * cos + pltpu.roll(v, HEAD_SIZE // 2, 1) * sin).astype(jnp.bfloat16)

    length = length_ref[0]
    own_keys = rope(pk_ref[...])
    own_values = pv_ref[...].astype(jnp.bfloat16)
    keys, values = keys_ref[...], values_ref[...]
    causal = lax.broadcasted_iota(jnp.int32, (rows, rows), 0) <= lax.broadcasted_iota(
        jnp.int32, (rows, rows), 1
    )
    active = lax.broadcasted_iota(jnp.int32, (rows, HEAD_SIZE), 0) < length
    active_t = lax.broadcasted_iota(jnp.int32, (HEAD_SIZE, rows), 1) < length
    grad_keys = jnp.zeros((prefix_length, HEAD_SIZE), jnp.float32)
    grad_values = jnp.zeros((prefix_length, HEAD_SIZE), jnp.float32)
    for g in range(GROUP):
        columns = slice(g * HEAD_SIZE, (g + 1) * HEAD_SIZE)
        query = rope(pq_ref[:, columns])
        upstream = jnp.where(active, cot_ref[:, columns].astype(jnp.float32), 0.0)
        upstream_t = upstream.T
        upstream = upstream.astype(jnp.bfloat16)
        pre = dot_f32(keys, query, 1, 1)
        own = jnp.where(causal, dot_f32(own_keys, query, 1, 1), -jnp.inf)
        highest = jnp.maximum(
            jnp.max(pre, axis=0, keepdims=True), jnp.max(own, axis=0, keepdims=True)
        )
        pre = jnp.exp2((pre - highest) * (scale * LOG2E))
        own = jnp.exp2((own - highest) * (scale * LOG2E))
        inverse = 1.0 / (
            jnp.sum(pre, axis=0, keepdims=True) + jnp.sum(own, axis=0, keepdims=True)
        )
        pre = pre * inverse
        pre_low = pre.astype(jnp.bfloat16)
        own_low = (own * inverse).astype(jnp.bfloat16)
        attended = dot_f32(values, pre_low, 0, 0) + dot_f32(own_values, own_low, 0, 0)
        attended = jnp.where(active_t, attended, 0.0).astype(jnp.bfloat16).astype(jnp.float32)
        delta = jnp.sum(upstream_t * attended, axis=0, keepdims=True)
        out_ref[:, columns] = attended.T.astype(jnp.bfloat16)
        dprob = dot_f32(values, upstream, 1, 1)
        dscore = (pre * (dprob - delta)).astype(jnp.bfloat16)
        grad_keys = grad_keys + dot_f32(dscore, query, 1, 0)
        grad_values = grad_values + dot_f32(pre_low, upstream, 1, 0)
    gk_ref[...] = (grad_keys * scale).astype(gk_ref.dtype)
    gv_ref[...] = grad_values.astype(gv_ref.dtype)


def attention(lengths, cos, sin, pq, pkv, prefix, cot, grad_dtype):
    rows, prefix_length = pq.shape[0], prefix.shape[0]
    d, kv = HEAD_SIZE, KEY_VALUE_HEADS
    full = pl.BlockSpec((rows, d), lambda h: (0, 0))
    key_block = lambda n: pl.BlockSpec((n, d), lambda h: (0, h))
    value_block = lambda n: pl.BlockSpec((n, d), lambda h: (0, h + kv))
    wide = pl.BlockSpec((rows, GROUP * d), lambda h: (0, h))
    grad = jax.ShapeDtypeStruct((prefix_length, kv * d), grad_dtype)
    return pl.pallas_call(
        attention_kernel,
        grid=(kv,),
        in_specs=[
            pl.BlockSpec(memory_space=pltpu.SMEM), full, full, wide,
            key_block(rows), value_block(rows),
            key_block(prefix_length), value_block(prefix_length), wide,
        ],
        out_specs=(wide, key_block(prefix_length), key_block(prefix_length)),
        out_shape=(jax.ShapeDtypeStruct((rows, QUERY_HEADS * d), jnp.bfloat16), grad, grad),
        compiler_params=pltpu.CompilerParams(vmem_limit_bytes=32 * 1024 * 1024),
        cost_estimate=pl.CostEstimate(
            flops=2 * QUERY_HEADS * rows * d * (5 * prefix_length + 2 * rows),
            bytes_accessed=10 * 1024 * 1024,
            transcendentals=QUERY_HEADS * rows * (prefix_length + rows),
        ),
        name="attention",
    )(lengths, cos, sin, pq, pkv, pkv, prefix, prefix, cot)


def add_rows(pieces, features):
    return (
        jnp.dot(features, pieces[0], preferred_element_type=jnp.float32),
        jnp.dot(features, pieces[1], preferred_element_type=jnp.float32),
    )


def on_device(
    hidden,
    norm_gain,
    query_weight,
    key_value_weight,
    lengths,
    cotangent,
    cartridge,
    adam_first_moment,
    adam_second_moment,
):
    sequence_rows = hidden.shape[1]
    states = hidden[0].astype(jnp.float32)
    normed = (
        states * lax.rsqrt(jnp.mean(states * states, axis=1, keepdims=True) + 1e-05) * norm_gain
    ).astype(jnp.bfloat16)
    exchanged = lax.all_to_all(normed[None], "fsdp", split_axis=2, concat_axis=0, tiled=True)
    pair_rows = exchanged.reshape(-1, exchanged.shape[2])
    part_query, part_keyval = add_rows(
        (
            lax.all_gather(query_weight, "dp", axis=0, tiled=True),
            lax.all_gather(key_value_weight, "dp", axis=0, tiled=True),
        ),
        pair_rows,
    )
    proj_query, project_key_value = (
        lax.psum_scatter(part_query, "fsdp", scatter_dimension=0, tiled=True),
        lax.psum_scatter(part_keyval, "fsdp", scatter_dimension=0, tiled=True),
    )
    shard_rows = cartridge.shape[0]
    prefix_length = shard_rows * lax.axis_size("owner")
    gathered_rows = lax.all_gather(cartridge.astype(jnp.bfloat16), "owner", axis=0, tiled=True)
    cos, sin = angle_tables(sequence_rows, prefix_length)
    attention_out, gradient_keys, gradient_values = attention(
        lengths, cos, sin, proj_query, project_key_value, gathered_rows, cotangent[0],
        jnp.float32,
    )
    prefix_gradient = jnp.concatenate([gradient_keys, gradient_values], axis=1)
    summed = lax.psum(prefix_gradient, ("fsdp", "dp", "owner"))
    owned_sum = lax.dynamic_slice_in_dim(
        summed, lax.axis_index("owner") * shard_rows, shard_rows, 0
    )
    new_cartridge, new_first, new_second = adam_update(
        cartridge, adam_first_moment, adam_second_moment, owned_sum
    )
    return (
        attention_out.reshape(1, sequence_rows, QUERY_HEADS * HEAD_SIZE),
        new_cartridge,
        new_first,
        new_second,
    )


def solution(mesh):
    placed = (
        P(("fsdp", "dp", "owner"), None, None),
        P(),
        P(("fsdp", "dp"), None),
        P(("fsdp", "dp"), None),
        P(("fsdp", "dp", "owner")),
        P(("fsdp", "dp", "owner"), None, None),
        P("owner", None),
        P("owner", None),
        P("owner", None),
    )
    return jax.shard_map(
        on_device,
        mesh=mesh,
        in_specs=placed,
        out_specs=(
            P(("fsdp", "dp", "owner"), None, None),
            P("owner", None),
            P("owner", None),
            P("owner", None),
        ),
        check_vma=False,
    )
```

time: 527 us -> 515 us (0.977)
  matrix products: 37 us -> 15.9 us
  Pallas kernels: 0 us -> 15.2 us
  local copies, waits for them, and re-layouts: 34.3 us -> 22.7 us
  waiting for transfers between devices: 402 us -> 413 us
  other arithmetic: 33.5 us -> 28.1 us
    dot_general x6 -> x0, matrix products: 21 us -> none  [the longest x1 9.08 us: on_device(): jnp.einsum('hgsp,shgd->phd', dscore, grouped_heads, preferred_element_typ...]
    pallas_call x0 -> x1, Pallas kernels: none -> 15.2 us  [attention(): pl.pallas_call(attention_kernel, grid=(kv,), in_specs=[pl.BlockSpec(memor...]
    unnamed x32 -> x26, local copies, waits for them, and re-layouts: 15.3 us -> 13 us
  transfers between devices with their start and end apart: 7 -> 7, of which waited for: 7 -> 7; matrix products, arithmetic and copies ran while one was open for 13% -> 11% of each run, Pallas kernels for 0% -> 0%
where the time goes in v1:
time: 515 us; the launch traced here: 514 us
  waiting for transfers between devices  413 us (80%)
  other arithmetic  28.1 us (5%)
  local copies, waits for them, and re-layouts  22.7 us (4%)
  matrix products  15.9 us (3%)
  Pallas kernels  15.2 us (3%)
  between operations  14.9 us (3%)
    all_gather x1, waiting for transfers between devices, on_device(): lax.all_gather(query_weight, 'dp', axis=0, tiled=True)  143 us
    psum x1, waiting for transfers between devices, on_device(): summed = lax.psum(prefix_gradient, ('fsdp', 'dp', 'owner'))  134 us
    reduce_scatter x1, waiting for transfers between devices, on_device(): lax.psum_scatter(part_query, 'fsdp', scatter_dimension=0, tiled=True)  56.6 us
    reduce_scatter x1, waiting for transfers between devices, on_device(): lax.psum_scatter(part_keyval, 'fsdp', scatter_dimension=0, tiled=True)  34 us
    all_to_all x1, waiting for transfers between devices, on_device(): lax.all_to_all(normed[None], 'fsdp', split_axis=2, concat_axis=0, tiled=T...  25.1 us
    unnamed x1, other arithmetic  21.7 us
    pallas_call x1, Pallas kernels, attention(): pl.pallas_call(attention_kernel, grid=(kv,), in_specs=[pl.BlockSpec(memor...  15.2 us
    unnamed x26, local copies, waits for them, and re-layouts  13 us
  transfers between devices with their start and end apart: 7, of which 7 were waited for; matrix products, arithmetic and copies ran while one was open for 11% of the time, Pallas kernels for 0%

profile of v1, /device:TPU:0, one launch (start us, length us, event | category | flops | bytes accessed | tf_op | source)
XLA Modules:
  0.0 514.5 jit_solution(1802552777185787782)
XLA Ops:
  7.2 0.7 all-gather.6.cloned.1.call-update
  8.0 0.7 all-gather.4.cloned.1.call-update
  8.8 0.5 fusion
  9.3 1.1 copy-done.5
  10.4 0.6 fusion.2
  11.0 7.3 %copy.17 = bf16[1,256,4096]{1,0,2:T(2,128)(2,1)} copy(bf16[1,256,4096]{2,1,0:T(8,128)(2,1)S(1)} %fusion.2) | data formatting | bytes 4194304 | tf_op jit(solution)/shard_map/convert_element_type | solution.py:150
  18.3 0.5 broadcast.34
  18.8 21.7 %reduce.1 = bf16[4096,256]{1,0:T(8,128)(2,1)S(1)} reduce(bf16[4096,1,256]{2,1,0:T(2,128)(2,1)} %bitcast.13, bf16[]{:T(256)} %broadcast.34), dimensions={1}, to_apply=%bitcast.6.reduce_sub_computation | reduce | bytes 4194306
  40.4 1.6 reshape.52
  42.1 4.3 all-to-all-start
  46.4 0.7 convert_element_type.28
  47.2 25.1 %all-to-all-done = bf16[2,2,262144]{2,1,0:T(2,128)(2,1)S(1)} async-done(((bf16[2,2,262144]{2,1,0:T(2,128)(2,1)}), bf16[2,2,262144]{2,1,0:T(2,128)(2,1)S(1)}, u32[]{:S(2)}, u32[]{:S(2)}) %all-to-all-start) | async-done | bytes 2097184 | tf_op jit(solution)/shard_map/all_to_all | solution.py:151
  72.2 3.1 reshape.53
  75.3 2.5 copy.19
  77.9 2.4 copy.18
  80.3 12.8 %all-gather.6.cloned.1.call-done = bf16[2048,1024]{1,0:T(8,128)(2,1)} async-done(((bf16[512,1024]{1,0:T(8,128)(2,1)}), bf16[2048,1024]{1,0:T(8,128)(2,1)}) %all-gather.6.cloned.1.call-update) | async-done | bytes 4194320 | tf_op jit(solution)/shard_map/all_gather | solution.py:156
  93.1 6.5 %fusion.7 = f32[512,1024]{1,0:T(8,128)} fusion(bf16[512,2048]{1,0:T(8,128)(2,1)} %bitcast.16, bf16[2048,1024]{1,0:T(8,128)(2,1)} %all-gather.6.cloned.1.call-done), kind=kOutput, calls=%fused_computation.19 | convolution fusion | flops 2147483648 | bytes 8388608 | tf_op jit(solution)/shard_map/dot_general | solution.py:131
  99.7 143.2 %all-gather.4.cloned.1.call-done = bf16[2048,2048]{1,0:T(8,128)(2,1)} async-done(((bf16[512,2048]{1,0:T(8,128)(2,1)}), bf16[2048,2048]{1,0:T(8,128)(2,1)}) %all-gather.4.cloned.1.call-update) | async-done | bytes 8388624 | tf_op jit(solution)/shard_map/all_gather | solution.py:155
  242.8 9.4 %fusion.6 = f32[512,2048]{1,0:T(8,128)} fusion(bf16[512,2048]{1,0:T(8,128)(2,1)S(1)} %bitcast.17, bf16[2048,2048]{1,0:T(8,128)(2,1)} %all-gather.4.cloned.1.call-done), kind=kOutput, calls=%fused_computation.18 | convolution fusion | flops 4294967296 | bytes 14680064 | tf_op jit(solution)/shard_map/dot_general | solution.py:130
  252.3 0.2 all-reduce.2.cloned.1.call-start
  253.2 0.5 fusion.4
  253.8 0.1 pad_maximum_fusion.1
  253.9 6.1 %all-gather.8.cloned.1.call-done.keys_ref.values_ref = bf16[512,1024]{1,0:T(8,128)(2,1)} async-done(((bf16[128,1024]{1,0:T(8,128)(2,1)}), bf16[512,1024]{1,0:T(8,128)(2,1)}) %all-gather.8.cloned.1.call-update) | async-done | bytes 1048592 | tf_op jit(solution)/shard_map/all_gather | solution.py:166
  260.0 34.0 %reduce-scatter.5.cloned.1.call-done.pk_ref.pv_ref = f32[256,1024]{1,0:T(8,128)} async-done(((f32[512,1024]{1,0:T(8,128)}), f32[256,1024]{1,0:T(8,128)}) %reduce-scatter.5.cloned.1.call-update) | async-done | bytes 1048592 | tf_op jit(solution)/shard_map/reduce_scatter | solution.py:162
  293.9 56.6 %reduce-scatter.3.cloned.1.call-done.pq_ref = f32[256,2048]{1,0:T(8,128)} async-done(((f32[512,2048]{1,0:T(8,128)}), f32[256,2048]{1,0:T(8,128)}) %reduce-scatter.3.cloned.1.call-update) | async-done | bytes 2097168 | tf_op jit(solution)/shard_map/reduce_scatter | solution.py:161
  350.5 1.6 copy-done
  352.1 1.2 copy-done.2
  353.4 1.2 copy-done.3
  354.6 15.2 %attention.1 = (bf16[256,2048]{1,0:T(8,128)(2,1)}, f32[512,512]{1,0:T(8,128)S(1)}, f32[512,512]{1,0:T(8,128)S(1)}) custom-call(s32[1]{0:T(128)S(6)} %copy.21.length_ref, f32[256,128]{1,0:T(8,128)S(1)} %get-tuple-element.16.cos_ref, f32[256,128]{1,0:T(8,128)S(1)} %get-tuple-element.17.sin_ref, f32[256,2048]{1,0:T(8,128)S(1)} %copy-done, ...), custom_call_target="tpu_custom_call" | custom-call | flops 3221225472 | bytes 10485760 | tf_op jit(solution)/shard_map/attention/pallas_call | solution.py:108
  369.8 1.5 pad_maximum_fusion
  371.3 133.9 %all-reduce.2.cloned.1.call-done = f32[512,1024]{1,0:T(8,128)} async-done(((f32[512,1024]{1,0:T(8,128)}), f32[512,1024]{1,0:T(8,128)}) %all-reduce.2.cloned.1.call-update) | async-done | bytes 2097168 | tf_op jit(solution)/shard_map/psum | solution.py:173
  505.3 2.4 divide_subtract_fusion
  (30 shorter events, 0.4 us)
Async XLA Ops:
  7.2 1.6 copy-start.4
  7.2 85.9 %all-gather.6.cloned.1.call-start = ((), (), s32[]{:S(2)}) async-start(), calls=%async_computation.5 | async-start | bytes 5242880 | tf_op jit(solution)/shard_map/all_gather | solution.py:156
  7.9 1.4 copy-start.10
  7.9 234.9 %all-gather.4.cloned.1.call-start = ((), (), s32[]{:S(2)}) async-start(), calls=%async_computation.3 | async-start | bytes 10485760 | tf_op jit(solution)/shard_map/all_gather | solution.py:155
  8.8 1.6 copy-start.5
  42.1 4.3 copy-start.7
  42.1 30.2 %all-to-all-start = ((bf16[2,2,262144]{2,1,0:T(2,128)(2,1)}), bf16[2,2,262144]{2,1,0:T(2,128)(2,1)S(1)}, u32[]{:S(2)}, u32[]{:S(2)}) async-start(bf16[2,2,262144]{2,1,0:T(2,128)(2,1)} %reshape.52), calls=%async_computation | async-start | bytes 4194304 | tf_op jit(solution)/shard_map/all_to_all | solution.py:151
  46.4 213.6 %all-gather.8.cloned.1.call-start = ((), (), s32[]{:S(2)}) async-start(), calls=%async_computation.7 | async-start | bytes 1310720 | tf_op jit(solution)/shard_map/all_gather | solution.py:166
  47.1 246.8 %reduce-scatter.5.cloned.1.call-start = ((), (), s32[]{:S(2)}) async-start(), calls=%async_computation.6 | async-start | bytes 3145728 | tf_op jit(solution)/shard_map/reduce_scatter | solution.py:162
  99.6 143.3 %copy-start.6 = (bf16[2,1,256,2048]{3,2,0,1:T(8,128)(2,1)S(1)}, bf16[2,1,256,2048]{3,2,0,1:T(8,128)(2,1)}, u32[]{:S(2)}) copy-start(bf16[2,1,256,2048]{3,2,0,1:T(8,128)(2,1)} %copy.18) | copy-start | bytes 6291460
  99.6 250.9 %reduce-scatter.3.cloned.1.call-start = ((), (), s32[]{:S(2)}) async-start(), calls=%async_computation.4 | async-start | bytes 6291456 | tf_op jit(solution)/shard_map/reduce_scatter | solution.py:161
  252.2 98.3 %copy-start.1 = (bf16[1,256,2048]{2,1,0:T(8,128)(2,1)S(1)}, bf16[1,256,2048]{2,1,0:T(8,128)(2,1)}, u32[]{:S(2)}) copy-start(bf16[1,256,2048]{2,1,0:T(8,128)(2,1)} %param.14) | copy-start | bytes 3145732
  252.3 253.0 %all-reduce.2.cloned.1.call-start = ((), (), s32[]{:S(2)}) async-start(), calls=%async_computation.8 | async-start | bytes 4194304 | tf_op jit(solution)/shard_map/psum | solution.py:173
  350.5 1.6 copy-start
  352.1 1.2 copy-start.2
  353.4 1.2 copy-start.3
  371.3 133.9 %copy-start.8 = (f32[128,1024]{1,0:T(8,128)S(1)}, f32[128,1024]{1,0:T(8,128)}, u32[]{:S(2)}) copy-start(f32[128,1024]{1,0:T(8,128)} %param.16) | copy-start | bytes 1572868
  371.3 133.9 %copy-start.9 = (f32[128,1024]{1,0:T(8,128)S(1)}, f32[128,1024]{1,0:T(8,128)}, u32[]{:S(2)}) copy-start(f32[128,1024]{1,0:T(8,128)} %param.17) | copy-start | bytes 1572868
Sparse Core Ops, SparseCore 0:
  9.6 83.4 all-gather.5
  94.6 148.1 all-gather.3
  245.0 14.9 all-gather.7
  262.1 31.8 reduce-scatter.4
  296.2 54.3 reduce-scatter.2
  371.5 133.7 all-reduce.1
